TPU v7x, 512 devices: a whole 4x4x16 slice. The times are simulated.
512 devices in a mesh: row: 32 (over x, y, core), col: 16 (over z).
Axes of the slice: x: 4, y: 4, z: 16, core: 2. Of those that a mesh axis runs over, the one named last changes fastest.
Arguments:
- tokens: bfloat16 [4096, 8192], P('row', 'col'), may hold values from -6 to 6
- gate_pre: bfloat16 [4096, 28672], P('col', 'row'), may hold values from -10 to 10
- grad_hidden: bfloat16 [4096, 28672], P('col', 'row'), may hold values from -6 to 6
- up_values: bfloat16 [28672, 8192], P('row', 'col'), may hold values from -0.03125 to 0.03125
- up_scales: float32 [224, 64], P('row', 'col'), may hold values from 0.5 to 2
- adapter_down: float32 [8192, 64], P('col'), may hold values from -0.0625 to 0.0625
- adapter_up: float32 [64, 28672], P(None, 'row'), may hold values from -0.03125 to 0.03125
- layer_gates: float32 [126], replicated, may hold values from 0.25 to 4
- layer: int32 [1], replicated, may hold values from 0 to 125
Outputs:
- grad_input: bfloat16 [4096, 8192], P('row', 'col')
- grad_down: float32 [8192, 64], P('col')
- grad_up: float32 [64, 28672], P(None, 'row')
- gate_grad: float32 [], replicated
All inputs are finite; a program needn't handle non-finite values.
Results may differ from a plain program's by a relative error of at most 0.02.
Values may be sent and summed in bfloat16 or wider, within the bound.
A program may use at most 64 MiB of HBM per device.

v0:
```python
import jax
import jax.numpy as jnp
from jax import lax
from jax.sharding import PartitionSpec as P

QBLOCK = 128


def per_device(
    tokens,
    gate_pre,
    grad_hidden,
    up_values,
    up_scales,
    adapter_down,
    adapter_up,
    layer_gates,
    layer,
):
    high = lax.Precision.HIGHEST
    gate_value = jnp.sum(
        jnp.where(
            jnp.arange(layer_gates.shape[0], dtype=jnp.int32) == layer[0],
            layer_gates,
            jnp.float32(0.0),
        )
    )
    grad_pre = (grad_hidden.astype(jnp.float32) * jax.nn.silu(gate_pre.astype(jnp.float32))).astype(
        jnp.bfloat16
    )
    expanded = jnp.repeat(jnp.repeat(up_scales, QBLOCK, axis=0), QBLOCK, axis=1)
    weights = (up_values.astype(jnp.float32) * expanded).astype(jnp.bfloat16)
    tok_rows = tokens.shape[0]
    tok_cols = grad_pre.shape[0]
    row_index = lax.axis_index("row")
    col_index = lax.axis_index("col")
    everyone = lax.all_gather(grad_pre, "col", axis=0, tiled=True)
    summed = lax.psum_scatter(
        jnp.dot(everyone, weights, preferred_element_type=jnp.float32).astype(jnp.bfloat16),
        "row",
        scatter_dimension=0,
        tiled=True,
    ).astype(jnp.float32)
    tokens_wide = tokens.astype(jnp.float32)
    grad_wide = grad_pre.astype(jnp.float32)
    z_part = jnp.dot(tokens_wide, adapter_down, precision=high)
    y_part = jnp.dot(grad_wide, adapter_up.T, precision=high)
    z_rows = lax.psum(z_part, "col")
    z_full = lax.all_gather(z_rows, "row", axis=0, tiled=True)
    y_cols = lax.psum(y_part, "row")
    y_full = lax.all_gather(y_cols, "col", axis=0, tiled=True)
    y_mine = lax.dynamic_slice_in_dim(y_full, row_index * tok_rows, tok_rows, 0)
    z_mine = lax.dynamic_slice_in_dim(z_full, col_index * tok_cols, tok_cols, 0)
    grad_input = (summed + gate_value * jnp.dot(y_mine, adapter_down.T, precision=high)).astype(
        jnp.bfloat16
    )
    down_part = gate_value * jnp.dot(tokens_wide.T, y_mine, precision=high)
    grad_down = lax.psum(down_part, "row")
    up_part = gate_value * jnp.dot(z_mine.T, grad_wide, precision=high)
    grad_up = lax.psum(up_part, "col")
    gate_grad = jnp.sum(z_full * y_full)
    return (grad_input, grad_down, grad_up, gate_grad)


def solution(mesh):
    placed = (
        P("row", "col"),
        P("col", "row"),
        P("col", "row"),
        P("row", "col"),
        P("row", "col"),
        P("col", None),
        P(None, "row"),
        P(),
        P(),
    )
    return jax.shard_map(
        per_device,
        mesh=mesh,
        in_specs=placed,
        out_specs=(P("row", "col"), P("col", None), P(None, "row"), P()),
        check_vma=False,
    )
```

profile of v0, /device:TPU:6, one launch (start us, length us, event | category | flops | bytes accessed | tf_op | source)
XLA Modules:
  0.0 597.7 jit_solution(5337956542964242562)
XLA Ops:
  8.0 0.0 copy-start
  8.0 0.0 copy-start.5
  8.0 0.0 all-reduce.4.cloned.1.call-start
  8.1 1.5 fusion.9
  9.6 0.0 copy-start.1
  9.6 0.0 copy-done
  9.6 1.1 fusion.17
  10.8 0.0 all-reduce.4.cloned.1.call-update
  10.8 0.0 all-gather.4.cloned.1.call-start
  10.8 0.0 copy-done.1
  10.9 0.5 all-gather.4.cloned.1.call-update
  11.4 0.0 all-gather.6.cloned.1.call-start
  11.4 132.2 %all-reduce.4.cloned.1.call-done = f32[256,64]{0,1:T(8,128)} async-done(((f32[256,64]{0,1:T(8,128)}), f32[256,64]{0,1:T(8,128)}) %all-reduce.4.cloned.1.call-update) | async-done | bytes 65552 | tf_op jit(solution)/shard_map/psum | solution.py:50
  143.6 0.0 all-gather.6.cloned.1.call-update
  143.6 0.0 all-gather.8.cloned.1.call-start
  143.7 1.2 fusion.18
  144.9 57.8 %psum.30 = f32[128,64]{0,1:T(8,128)} all-reduce(f32[128,64]{0,1:T(8,128)S(1)} %fusion.18), channel_id=1, replica_groups=mesh['row'=32,'col'=16] {'col'}, use_global_device_ids=true, to_apply=%region_4.5 | all-reduce | flops 8192 | bytes 65536 | tf_op jit(solution)/shard_map/psum | solution.py:48
  202.7 0.0 all-gather.8.cloned.1.call-update
  202.7 0.0 reduce-scatter.2.cloned.1.call-start
  202.7 0.8 copy.13
  203.5 0.0 all-gather.4.cloned.1.call-done
  203.5 1.1 broadcast_in_dim.11
  204.7 0.0 copy-done.5
  204.7 9.4 %convolution_convert_fusion = bf16[4096,512]{1,0:T(8,128)(2,1)} fusion(bf16[4096,896]{1,0:T(8,128)(2,1)} %all-gather.4.cloned.1.call-done, f32[112,8,4,128]{3,2,1,0:T(4,128)S(1)} %bitcast.19, bf16[896,512]{1,0:T(8,128)(2,1)S(1)} %copy-done.5), kind=kOutput, calls=%fused_computation | convolution fusion | flops 3761569792 | bytes 14286848 | tf_op jit(solution)/shard_map/dot_general | solution.py:39
  214.0 0.0 copy-start.6
  214.0 0.0 copy-start.3
  214.0 0.0 copy-start.2
  214.0 0.0 reduce-scatter.2.cloned.1.call-update
  214.1 0.0 all-reduce.6.cloned.1.call-start
  214.8 0.0 copy-done.6
  214.9 0.7 fusion.13
  215.5 0.0 all-gather.6.cloned.1.call-done
  215.5 0.0 copy-done.3
  215.5 2.3 fusion.3
  217.8 0.0 all-reduce.6.cloned.1.call-update
  217.8 0.0 all-reduce.8.cloned.1.call-start
  217.9 56.1 %all-gather.8.cloned.1.call-done = f32[4096,64]{0,1:T(8,128)} async-done(((f32[128,64]{0,1:T(8,128)}), f32[4096,64]{0,1:T(8,128)}) %all-gather.8.cloned.1.call-update) | async-done | bytes 1048592 | tf_op jit(solution)/shard_map/all_gather | solution.py:49
  274.0 0.0 copy-done.2
  274.0 2.6 convolution_multiply_fusion.1
  276.5 0.0 all-reduce.8.cloned.1.call-update
  276.6 2.5 multiply_reduce_fusion
  279.0 35.8 %reduce-scatter.2.cloned.1.call-done = bf16[128,512]{1,0:T(8,128)(2,1)} async-done(((bf16[4096,512]{1,0:T(8,128)(2,1)}), bf16[128,512]{1,0:T(8,128)(2,1)}) %reduce-scatter.2.cloned.1.call-update) | async-done | bytes 131088 | tf_op jit(solution)/shard_map/reduce_scatter | solution.py:38
  314.9 0.0 copy-done.4
  314.9 2.7 fusion.2
  317.6 132.2 %all-reduce.6.cloned.1.call-done = f32[512,64]{0,1:T(8,128)} async-done(((f32[512,64]{0,1:T(8,128)}), f32[512,64]{0,1:T(8,128)}) %all-reduce.6.cloned.1.call-update) | async-done | bytes 131088 | tf_op jit(solution)/shard_map/psum | solution.py:58
  449.7 137.4 %all-reduce.8.cloned.1.call-done = f32[64,896]{1,0:T(8,128)} async-done(((f32[64,896]{1,0:T(8,128)}), f32[64,896]{1,0:T(8,128)}) %all-reduce.8.cloned.1.call-update) | async-done | bytes 229392 | tf_op jit(solution)/shard_map/psum | solution.py:60
  587.1 1.6 copy.21
  588.7 1.6 copy.22
  (2 shorter events, 0.0 us)
Async XLA Ops:
  8.0 1.6 copy-start
  8.0 196.6 %copy-start.5 = (bf16[896,512]{1,0:T(8,128)(2,1)S(1)}, bf16[896,512]{1,0:T(8,128)(2,1)}, u32[]{:S(2)}) copy-start(bf16[896,512]{1,0:T(8,128)(2,1)} %param.12) | copy-start | bytes 2752516
  8.0 135.6 %all-reduce.4.cloned.1.call-start = ((), (), s32[]{:S(2)}) async-start(), calls=%async_computation.3 | async-start | bytes 131072 | tf_op jit(solution)/shard_map/psum | solution.py:50
  9.6 1.2 copy-start.1
  10.8 192.7 %all-gather.4.cloned.1.call-start = ((), (), s32[]{:S(2)}) async-start(), calls=%async_computation.1 | async-start | bytes 7798784 | tf_op jit(solution)/shard_map/all_gather | solution.py:37
  11.4 204.2 %all-gather.6.cloned.1.call-start = ((), (), s32[]{:S(2)}) async-start(), calls=%async_computation.4 | async-start | bytes 1114112 | tf_op jit(solution)/shard_map/all_gather | solution.py:51
  143.6 130.3 %all-gather.8.cloned.1.call-start = ((), (), s32[]{:S(2)}) async-start(), calls=%async_computation.6 | async-start | bytes 1081344 | tf_op jit(solution)/shard_map/all_gather | solution.py:49
  202.7 112.2 %reduce-scatter.2.cloned.1.call-start = ((), (), s32[]{:S(2)}) async-start(), calls=%async_computation.2 | async-start | bytes 4325376 | tf_op jit(solution)/shard_map/reduce_scatter | solution.py:38
  214.0 0.8 copy-start.6
  214.0 1.5 copy-start.3
  214.0 59.9 %copy-start.2 = (bf16[256,896]{1,0:T(8,128)(2,1)S(1)}, bf16[256,896]{1,0:T(8,128)(2,1)}, u32[]{:S(2)}) copy-start(bf16[256,896]{1,0:T(8,128)(2,1)} %copy-done.1) | copy-start | bytes 1376260
  214.0 100.8 %copy-start.4 = (f32[512,64]{0,1:T(8,128)S(1)}, f32[512,64]{0,1:T(8,128)}, u32[]{:S(2)}) copy-start(f32[512,64]{0,1:T(8,128)} %param.14) | copy-start | bytes 393220
  214.1 235.7 %all-reduce.6.cloned.1.call-start = ((), (), s32[]{:S(2)}) async-start(), calls=%async_computation.5 | async-start | bytes 262144 | tf_op jit(solution)/shard_map/psum | solution.py:58
  217.8 369.3 %all-reduce.8.cloned.1.call-start = ((), (), s32[]{:S(2)}) async-start(), calls=%async_computation.7 | async-start | bytes 458752 | tf_op jit(solution)/shard_map/psum | solution.py:60
Sparse Core Ops, SparseCore 0:
  12.7 130.8 all-reduce.3
  214.2 100.6 reduce-scatter.1
  318.7 131.0 all-reduce.5
  452.6 134.4 all-reduce.7
Sparse Core Ops, SparseCore 1:
  13.6 99.7 all-gather.3
  143.7 71.1 all-gather.5
  218.8 55.1 all-gather.7
where the time goes:
time: 598 us
  waiting for transfers between devices  494 us (83%)
  blocking collectives  57.8 us (10%)
  matrix products  19.3 us (3%)
  between operations  16.3 us (3%)
    psum x1, waiting for transfers between devices, per_device(): grad_up = lax.psum(up_part, 'col')  137 us
    psum x1, waiting for transfers between devices, per_device(): y_cols = lax.psum(y_part, 'row')  132 us
    psum x1, waiting for transfers between devices, per_device(): grad_down = lax.psum(down_part, 'row')  132 us
    psum x1, blocking collectives, per_device(): z_rows = lax.psum(z_part, 'col')  57.8 us
    all_gather x1, waiting for transfers between devices, per_device(): z_full = lax.all_gather(z_rows, 'row', axis=0, tiled=True)  56.1 us
    reduce_scatter x1, waiting for transfers between devices, per_device(): lax.psum_scatter(jnp.dot(everyone, weights, preferred_element_type=jnp.fl...  35.8 us
  transfers between devices with their start and end apart: 7, of which 5 were waited for; matrix products, arithmetic and copies ran while one was open for 4% of the time, Pallas kernels for 0%

commit v1 on v0

v1 whole, which is shorter than its diff:
```python
import functools

import jax
import jax.numpy as jnp
from jax import lax
from jax.experimental import pallas as pl
from jax.experimental.pallas import tpu as pltpu
from jax.sharding import PartitionSpec as P

QBLOCK = 128
MESH = pl.DeviceIdType.MESH
F32 = jnp.float32
BF16 = jnp.bfloat16


def split_rows(v):
    high = v.astype(BF16)
    low = (v - high.astype(F32)).astype(BF16)
    return jnp.concatenate([high, low], axis=0)


def fold_rows(v):
    half = v.shape[0] // 2
    return v[:half] + v[half:]


def dot_nt(a, b):
    return lax.dot_general(a, b, (((1,), (1,)), ((), ())), preferred_element_type=F32)


def dot_nn(a, b):
    return jnp.dot(a, b, preferred_element_type=F32)


def kernel(
    n_row,
    n_col,
    tok_ref,
    gate_ref,
    hid_ref,
    up_ref,
    scale_ref,
    down_ref,
    adup_ref,
    gates_ref,
    layer_ref,
    gi_ref,
    gd_ref,
    gu_ref,
    gg_ref,
    gbuf,
    wbuf,
    stage,
    rbuf,
    ost,
    fin,
    lora,
    zst,
    zrb,
    zfull,
    zcat,
    yst,
    yrb,
    y2st,
    yt,
    gst,
    grb,
    gfull,
    sst,
    srb,
    gacc,
    ring_send,
    ring_recv,
    rs_send,
    rs_recv,
    sm_send,
    sm_recv,
):
    r = lax.axis_index("row")
    c = lax.axis_index("col")
    tr, dl = gi_ref.shape
    fl = gbuf.shape[3]
    rank = gd_ref.shape[1]
    n_pc = rank // 8
    half = n_col // 2
    cgs = dl // 128
    Z1, Z2, Z3, Y1, Y2, Y3, D1, D2, S1, FIN = range(10)

    def rcopy(src, dst, ssem, rsem, dev):
        return pltpu.make_async_remote_copy(
            src_ref=src, dst_ref=dst, send_sem=ssem, recv_sem=rsem, device_id=dev, device_id_type=MESH
        )

    def small(src, dst, which, dev):
        return rcopy(src, dst, sm_send.at[which], sm_recv.at[which], dev)

    def plane_peer(i):
        return (lax.rem(r + i, n_row), c)

    def col_peer(i):
        return (r, lax.rem(c + i, n_col))

    def each(low, high, fn):
        def body(i, carry):
            fn(i)
            return carry

        lax.fori_loop(low, high, body, 0)

    barrier = pltpu.get_barrier_semaphore()

    def hello(dev):
        pl.semaphore_signal(barrier, inc=1, device_id=dev, device_id_type=MESH)

    each(1, n_col, lambda i: hello(col_peer(i)))
    each(1, n_row, lambda i: hello(plane_peer(i)))
    even_c = lax.rem(c, 2) == 0
    odd_r = lax.rem(r, 2) == 1
    my_k = c // 2

    @pl.when(even_c)
    def _():
        hello((4 * my_k + 2 * lax.rem(r, 2) + 1, r // 2))

    for h in range(2):
        v = gate_ref[pl.ds(h * tr, tr), :].astype(F32)
        g = hid_ref[pl.ds(h * tr, tr), :].astype(F32) * (v / (1.0 + jnp.exp(-v)))
        gbuf[c, h] = g.astype(BF16)

    @pl.when(odd_r)
    def _():
        pl.semaphore_wait(barrier, n_col + n_row - 1)

    @pl.when(jnp.logical_not(odd_r))
    def _():
        pl.semaphore_wait(barrier, n_col + n_row - 2)

    right = lax.rem(c + 1, n_col)
    left = lax.rem(c + n_col - 1, n_col)

    def ring(way, s, h):
        if way == 0:
            block, dev = lax.rem(c - s + n_col, n_col), (r, right)
        else:
            block, dev = lax.rem(c + s, n_col), (r, left)
        part = gbuf.at[block, h]
        return rcopy(part, part, ring_send.at[way, s, h], ring_recv.at[way, s, h], dev)

    for h in range(2):
        for way in range(2):
            ring(way, 0, h).start()

    gv = gates_ref[layer_ref[0]]
    a_t = down_ref[...].T
    zst[...] = fold_rows(dot_nt(split_rows(a_t), tok_ref[...])).reshape(n_pc, 8, tr)

    def z1(k):
        @pl.when(2 * k != c)
        def _():
            small(zst.at[k], zrb.at[c], Z1, (r, 2 * k)).start()

    each(0, n_pc, z1)

    own = gbuf[c].reshape(2 * tr, fl)
    y_part = fold_rows(dot_nt(split_rows(adup_ref[...]), own))
    for k in range(n_pc):
        for h in range(2):
            yst[2 * k + h] = y_part[8 * k : 8 * k + 8, h * tr : (h + 1) * tr]

    def y1(i):
        @pl.when(2 * i + 1 != r)
        def _():
            small(yst.at[i], yrb.at[r], Y1, (2 * i + 1, c)).start()

    each(0, 2 * n_pc, y1)

    for i in range(fl // QBLOCK):
        for j in range(dl // QBLOCK):
            at = (pl.ds(i * QBLOCK, QBLOCK), pl.ds(j * QBLOCK, QBLOCK))
            wbuf[at] = (up_ref[at].astype(F32) * scale_ref[i, j]).astype(BF16)

    def multiply(block, group, at):
        p = dot_nn(gbuf[block].reshape(2 * tr, fl), wbuf[...]).astype(BF16)
        for h in range(2):
            for tg in range(tr // 16):
                for cg in range(cgs):
                    stage[group, tg * cgs + cg, at + h] = p[
                        h * tr + 16 * tg : h * tr + 16 * tg + 16, 128 * cg : 128 * cg + 128
                    ]

    def scatter(group, parts):
        def send(i):
            j = lax.rem(r + i, n_row)
            rcopy(
                stage.at[group, j, pl.ds(0, parts)],
                rbuf.at[group, r, pl.ds(0, parts)],
                rs_send.at[group],
                rs_recv.at[group],
                (j, c),
            ).start()

        each(1, n_row, send)
        rbuf[group, r, pl.ds(0, parts)] = stage[group, r, pl.ds(0, parts)]

    def reduce(group, parts, blocks):
        got = rbuf.at[group, pl.ds(0, n_row - 1), pl.ds(0, parts)]
        rcopy(got, got, rs_send.at[group], rs_recv.at[group], (r, right)).wait_recv()

        def add(i, acc):
            return acc + rbuf[group, i, pl.ds(0, parts)].astype(F32)

        total = lax.fori_loop(0, n_row, add, jnp.zeros((parts, 16, 128), F32))
        ost[group, pl.ds(0, parts)] = total.astype(BF16)
        for part in range(parts):
            dest = 2 * blocks[part // 2] + part % 2

            @pl.when(dest != r)
            def _():
                small(ost.at[group, part], fin.at[r], FIN, (dest, c)).start()

            @pl.when(dest == r)
            def _():
                fin[r] = ost[group, part]

    def blocks_of(s):
        return (lax.rem(c - s + n_col, n_col), lax.rem(c + s, n_col))

    multiply(c, 0, 0)
    scatter(0, 2)

    def wait_small(which, ref):
        small(ref, ref, which, (r, right)).wait_recv()

    def hook_z1_y1():
        @pl.when(even_c)
        def _():
            zrb[c] = zst[my_k]
            wait_small(Z1, zrb.at[pl.ds(0, n_col - 1)])
            zfull[r, my_k] = jnp.sum(zrb[...], axis=0)
            each(1, n_col, lambda i: small(zfull.at[r, my_k], zfull.at[r, my_k], Z2, col_peer(i)).start())

        @pl.when(odd_r)
        def _():
            i = r // 2
            yrb[r] = yst[i]
            wait_small(Y1, yrb.at[pl.ds(0, n_row - 1)])
            y2st[...] = jnp.sum(yrb[...], axis=0)
            k = i // 2
            small(y2st, yt.at[k], Y2, (2 * c + lax.rem(i, 2), 2 * k)).start()

    def wait_pieces(which, ref):
        @pl.when(even_c)
        def _():
            if n_pc > 1:
                wait_small(which, ref.at[pl.ds(0, n_pc - 1)])

        @pl.when(jnp.logical_not(even_c))
        def _():
            wait_small(which, ref.at[pl.ds(0, n_pc)])

    def hook_z2_y2():
        wait_pieces(Z2, zfull.at[r])
        each(1, n_row, lambda i: small(zfull.at[r], zfull.at[r], Z3, plane_peer(i)).start())

        @pl.when(even_c)
        def _():
            wait_small(Y2, yt.at[my_k])
            each(1, n_col, lambda i: small(yt.at[my_k], yt.at[my_k], Y3, col_peer(i)).start())

    def hook_y3():
        wait_pieces(Y3, yt)
        y_t = yt[...].reshape(rank, tr)
        gd_t = fold_rows(dot_nn(split_rows(y_t), tok_ref[...]))
        for k in range(n_pc):
            for q in range(cgs):
                gst[k * cgs + q] = gd_t[8 * k : 8 * k + 8, 128 * q : 128 * q + 128]

        def send(i):
            j = lax.rem(r + i, n_row)
            small(gst.at[j], grb.at[r], D1, (j, c)).start()

        each(1, n_row, send)
        grb[r] = gst[r]

    def hook_lora():
        y_s = split_rows(yt[...].reshape(rank, tr))
        a_s = split_rows(down_ref[...].T)
        y_left = jnp.concatenate([y_s[:rank], y_s[:rank], y_s[rank:]], axis=0).astype(F32).T.astype(BF16)
        a_right = jnp.concatenate([a_s[:rank], a_s[rank:], a_s[:rank]], axis=0)
        lora[...] = gv * dot_nn(y_left, a_right)

    def hook_d1():
        wait_small(D1, grb.at[pl.ds(0, n_row - 1)])
        gfull[r] = jnp.sum(grb[...], axis=0)
        each(1, n_row, lambda i: small(gfull.at[r], gfull.at[r], D2, plane_peer(i)).start())

    def hook_d2():
        wait_small(D2, gfull.at[pl.ds(0, n_row - 1)])
        rows = []
        for k in range(n_pc):
            rows.append(jnp.concatenate([gfull[k * cgs + q] for q in range(cgs)], axis=1))
        gd_t = jnp.concatenate(rows, axis=0)
        gd_ref[...] = gv * gd_t.T
        total = jnp.sum(gd_t * down_ref[...].T)
        sst[...] = jnp.full(sst.shape, total, F32)
        srb[c] = sst[...]
        each(1, n_col, lambda i: small(sst, srb.at[c], S1, col_peer(i)).start())

    def hook_z3():
        wait_small(Z3, zfull.at[pl.ds(0, n_row - 1)])

        def one(b):
            z_t = jnp.concatenate(
                [zfull[2 * b].reshape(rank, tr), zfull[2 * b + 1].reshape(rank, tr)], axis=1
            )
            zcat[b] = split_rows(z_t)

        each(0, n_col, one)

    def hook_s1():
        wait_small(S1, srb.at[pl.ds(0, n_col - 1)])
        gg_ref[0, 0] = jnp.sum(jnp.sum(srb[...], axis=0)[0:1, 0:1])

    hooks = [
        (hook_z1_y1,),
        (hook_z2_y2,),
        (hook_y3,),
        (hook_d1, hook_lora),
        (hook_d2,),
        (hook_z3,),
        (hook_s1,),
    ]

    def step(s):
        ups, downs = blocks_of(s)

        for way in range(2):
            ring(way, s - 1, 0).wait_recv()
            if way == 0:
                ring(way, s, 0).start()
            else:
                pl.when(s < half - 1)(lambda: ring(1, s, 0).start())

        before = blocks_of(s - 1)

        @pl.when(s == 1)
        def _():
            reduce(0, 2, (c,))

        @pl.when(s > 1)
        def _():
            reduce(s - 1, 4, before)

        for at, some in enumerate(hooks):
            if at + 1 < half:

                @pl.when(s == at + 1)
                def _():
                    for hook in some:
                        hook()

        for way in range(2):
            ring(way, s - 1, 1).wait_recv()
            if way == 1:
                ring(way, s, 1).start()
            else:
                pl.when(s < half - 1)(lambda: ring(0, s, 1).start())

        multiply(ups, s, 0)
        multiply(downs, s, 2)
        scatter(s, 4)

    each(1, half, step)
    for at, some in enumerate(hooks):
        if at + 1 >= half:
            for hook in some:
                hook()

    reduce(half - 1, 4, blocks_of(half - 1))
    far = lax.rem(c + half, n_col)
    ring(0, half - 1, 0).wait_recv()
    ring(1, half - 1, 1).wait_recv()
    multiply(far, half, 0)
    scatter(half, 2)

    gacc[...] = jnp.zeros_like(gacc)

    def up_block(b):
        gacc[...] += dot_nn(zcat[b], gbuf[b].reshape(2 * tr, fl))

    each(0, n_col, up_block)
    gu_ref[...] = gv * fold_rows(gacc[...])

    reduce(half, 2, (far,))
    wait_small(FIN, fin.at[pl.ds(0, n_row - 1)])
    for tg in range(tr // 16):
        for cg in range(cgs):
            at = (pl.ds(16 * tg, 16), pl.ds(128 * cg, 128))
            gi_ref[at] = (fin[tg * cgs + cg].astype(F32) + lora[at]).astype(BF16)

    def drain(s):
        for way in range(2):
            for h in range(2):
                if way == h:
                    ring(way, s, h).wait_send()
                else:
                    pl.when(s < half - 1)(lambda: ring(way, s, h).wait_send())

    each(0, half, drain)

    def sent_group(group, parts):
        out = stage.at[group, pl.ds(0, n_row - 1), pl.ds(0, parts)]
        rcopy(out, out, rs_send.at[group], rs_recv.at[group], (r, right)).wait_send()

    sent_group(0, 2)
    each(1, half, lambda s: sent_group(s, 4))
    sent_group(half, 2)

    def sent(which, ref):
        small(ref, ref, which, (r, right)).wait_send()

    @pl.when(even_c)
    def _():
        if n_pc > 1:
            sent(Z1, zst.at[pl.ds(0, n_pc - 1)])
        sent(Z2, zrb.at[pl.ds(0, n_col - 1)])
        sent(Y3, zrb.at[pl.ds(0, n_col - 1)])

    @pl.when(jnp.logical_not(even_c))
    def _():
        sent(Z1, zst)

    @pl.when(odd_r)
    def _():
        sent(Y1, yst.at[pl.ds(0, 2 * n_pc - 1)])
        sent(Y2, y2st)

    @pl.when(jnp.logical_not(odd_r))
    def _():
        sent(Y1, yst)

    sent(Z3, zfull.at[pl.ds(0, n_row - 1)])
    sent(D1, gst.at[pl.ds(0, n_row - 1)])
    sent(D2, gfull.at[pl.ds(0, n_row - 1)])
    sent(S1, srb.at[pl.ds(0, n_col - 1)])
    sent(FIN, fin.at[pl.ds(0, 2 * n_col - 1)])


def per_device(
    n_row,
    n_col,
    tokens,
    gate_pre,
    grad_hidden,
    up_values,
    up_scales,
    adapter_down,
    adapter_up,
    layer_gates,
    layer,
):
    tr, dl = tokens.shape
    fl = up_values.shape[0]
    rank = adapter_down.shape[1]
    n_pc = rank // 8
    groups = n_col // 2 + 1
    vmem = pl.BlockSpec(memory_space=pltpu.VMEM)
    smem = pl.BlockSpec(memory_space=pltpu.SMEM)
    outs = pl.pallas_call(
        functools.partial(kernel, n_row, n_col),
        out_shape=(
            jax.ShapeDtypeStruct((tr, dl), BF16),
            jax.ShapeDtypeStruct((dl, rank), F32),
            jax.ShapeDtypeStruct((rank, fl), F32),
            jax.ShapeDtypeStruct((1, 1), F32),
        ),
        in_specs=[vmem, vmem, vmem, vmem, smem, vmem, vmem, smem, smem],
        out_specs=(vmem, vmem, vmem, smem),
        scratch_shapes=[
            pltpu.VMEM((n_col, 2, tr, fl), BF16),
            pltpu.VMEM((fl, dl), BF16),
            pltpu.VMEM((groups, n_row, 4, 16, 128), BF16),
            pltpu.VMEM((groups, n_row, 4, 16, 128), BF16),
            pltpu.VMEM((groups, 4, 16, 128), BF16),
            pltpu.VMEM((n_row, 16, 128), BF16),
            pltpu.VMEM((tr, dl), F32),
            pltpu.VMEM((n_pc, 8, tr), F32),
            pltpu.VMEM((n_col, 8, tr), F32),
            pltpu.VMEM((n_row, n_pc, 8, tr), F32),
            pltpu.VMEM((n_col, 2 * rank, 2 * tr), BF16),
            pltpu.VMEM((2 * n_pc, 8, tr), F32),
            pltpu.VMEM((n_row, 8, tr), F32),
            pltpu.VMEM((8, tr), F32),
            pltpu.VMEM((n_pc, 8, tr), F32),
            pltpu.VMEM((n_row, 8, 128), F32),
            pltpu.VMEM((n_row, 8, 128), F32),
            pltpu.VMEM((n_row, 8, 128), F32),
            pltpu.VMEM((8, 128), F32),
            pltpu.VMEM((n_col, 8, 128), F32),
            pltpu.VMEM((2 * rank, fl), F32),
            pltpu.SemaphoreType.DMA((2, n_col // 2, 2)),
            pltpu.SemaphoreType.DMA((2, n_col // 2, 2)),
            pltpu.SemaphoreType.DMA((groups,)),
            pltpu.SemaphoreType.DMA((groups,)),
            pltpu.SemaphoreType.DMA((10,)),
            pltpu.SemaphoreType.DMA((10,)),
        ],
        compiler_params=pltpu.CompilerParams(
            collective_id=0, has_side_effects=True, vmem_limit_bytes=48 * 1024 * 1024
        ),
    )(
        tokens,
        gate_pre,
        grad_hidden,
        up_values,
        up_scales,
        adapter_down,
        adapter_up,
        layer_gates,
        layer,
    )
    grad_input, grad_down, grad_up, gate_grad = outs
    return grad_input, grad_down, grad_up, gate_grad.reshape(())


def solution(mesh):
    placed = (
        P("row", "col"),
        P("col", "row"),
        P("col", "row"),
        P("row", "col"),
        P("row", "col"),
        P("col", None),
        P(None, "row"),
        P(),
        P(),
    )
    return jax.shard_map(
        functools.partial(per_device, mesh.shape["row"], mesh.shape["col"]),
        mesh=mesh,
        in_specs=placed,
        out_specs=(P("row", "col"), P("col", None), P(None, "row"), P()),
        check_vma=False,
    )
```

time: 598 us -> 141 us (0.24)
  the two profiles are of different devices: /device:TPU:6 before, /device:TPU:4 now
where the time goes in v1:
time: 141 us
  Pallas kernels  130 us (92%)
  local copies, waits for them, and re-layouts  7.17 us (5%)
  between operations  3.2 us (2%)
    pallas_call x1, Pallas kernels, per_device(): pl.pallas_call(functools.partial(kernel, n_row, n_col), out_shape=(jax.Sh...  130 us
    unnamed x17, local copies, waits for them, and re-layouts  7.17 us

profile of v1, /device:TPU:4, one launch (start us, length us, event | category | flops | bytes accessed | tf_op | source)
XLA Modules:
  0.0 140.6 jit_solution(4273510221251205621)
XLA Ops:
  0.6 0.0 copy-start.3
  1.3 0.8 copy.13.scale_ref
  2.1 0.0 copy-start.4
  2.1 0.0 copy-start.5
  2.1 1.1 copy.14.down_ref
  3.2 0.0 copy-done.3
  3.2 0.0 copy-done.4
  3.2 0.0 copy-done.5
  3.2 0.0 copy-start
  3.2 1.2 copy-done
  4.4 0.0 copy-start.1
  4.4 1.0 copy-done.1
  5.4 0.0 copy-start.2
  5.4 1.0 copy-done.2
  6.4 130.3 %shard_map.120 = (bf16[128,512]{1,0:T(8,128)(2,1)S(1)}, f32[512,64]{1,0:T(8,128)S(1)}, f32[64,896]{1,0:T(8,128)S(1)}, f32[1,1]{1,0:T(1,128)}) custom-call(bf16[128,512]{1,0:T(8,128)(2,1)S(1)} %copy-done.4, bf16[256,896]{1,0:T(8,128)(2,1)S(1)} %copy-done.1, bf16[256,896]{1,0:T(8,128)(2,1)S(1)} %copy-done.2, bf16[896,512]{1,0:T(8,128)(2,1)S(1)} %copy-done, ...), custom_call_target="tpu_custom_call" | custom-call | tf_op jit(solution)/shard_map/pallas_call | solution.py:469
  136.7 0.8 copy.15
  137.5 0.7 copy.20
  138.1 0.7 copy.21
Async XLA Ops:
  0.6 2.5 %copy-start.3 = (f32[64,896]{1,0:T(8,128)S(1)}, f32[64,896]{1,0:T(8,128)}, u32[]{:S(2)}) copy-start(f32[64,896]{1,0:T(8,128)} %adup_ref.1) | copy-start | bytes 688132
  2.1 1.1 copy-start.4
  2.1 1.1 copy-start.5
  3.2 1.2 copy-start
  4.4 1.0 copy-start.1
  5.4 1.0 copy-start.2

commit v2 on v1

v2 whole, which is shorter than its diff:
```python
import functools

import jax
import jax.numpy as jnp
from jax import lax
from jax.experimental import pallas as pl
from jax.experimental.pallas import tpu as pltpu
from jax.sharding import PartitionSpec as P

QBLOCK = 128
SUB = 4
MESH = pl.DeviceIdType.MESH
F32 = jnp.float32
BF16 = jnp.bfloat16
Z1, Z2, Z3, Y1, Y2, Y3, D1, D2, S1, FIN = range(10)


def split_rows(v):
    high = v.astype(BF16)
    low = (v - high.astype(F32)).astype(BF16)
    return jnp.concatenate([high, low], axis=0)


def fold_rows(v):
    half = v.shape[0] // 2
    return v[:half] + v[half:]


def dot_nt(a, b):
    return lax.dot_general(a, b, (((1,), (1,)), ((), ())), preferred_element_type=F32)


def dot_nn(a, b):
    return jnp.dot(a, b, preferred_element_type=F32)


def each(low, high, fn):
    def body(i, carry):
        fn(i)
        return carry

    lax.fori_loop(low, high, body, 0)


def kernel(
    n_row,
    n_col,
    tok_hbm,
    gate_hbm,
    hid_hbm,
    up_hbm,
    scale_ref,
    down_hbm,
    adup_hbm,
    gates_ref,
    layer_ref,
    gi_ref,
    gd_ref,
    gu_ref,
    gg_ref,
    tok,
    gate,
    hid,
    up,
    a_t,
    adup,
    gbuf,
    wbuf,
    keep,
    xst,
    xrb,
    stage,
    rbuf,
    ost,
    fin,
    lora,
    zst,
    zrb,
    zfull,
    zcat,
    gpart,
    yst,
    yrb,
    y2st,
    yt,
    gst,
    grb,
    gfull,
    srb,
    load_sem,
    ring_send,
    ring_recv,
    x_send,
    x_recv,
    rs_send,
    rs_recv,
    sm_send,
    sm_recv,
):
    r = lax.axis_index("row")
    c = lax.axis_index("col")
    core = lax.rem(r, 2)
    chip = lax.div(r, 2)
    tr, dl = gi_ref.shape
    fl = wbuf.shape[0]
    rank = gd_ref.shape[0]
    sub = 2 * tr // SUB
    n_pc = rank // 8
    n_chip = n_row // 2
    half = n_col // 2
    cgs = dl // 128
    tgs = n_chip // cgs
    right = lax.rem(c + 1, n_col)
    left = lax.rem(c + n_col - 1, n_col)
    odd = core == 1
    n_zp = rank // 16
    z_gap = n_col // n_zp
    z_owner = lax.rem(c, z_gap) == 0
    y_owner = lax.rem(c, 2) == 0
    my_z, my_k = lax.div(c, z_gap), lax.div(c, 2)

    def rcopy(src, dst, ssem, rsem, dev):
        return pltpu.make_async_remote_copy(
            src_ref=src, dst_ref=dst, send_sem=ssem, recv_sem=rsem, device_id=dev, device_id_type=MESH
        )

    def small(src, dst, which, dev):
        return rcopy(src, dst, sm_send.at[which], sm_recv.at[which], dev)

    def wait_small(which, ref):
        small(ref, ref, which, (r, right)).wait_recv()

    def sent(which, ref):
        small(ref, ref, which, (r, right)).wait_send()

    def plane_peer(i):
        return (lax.rem(r + i, n_row), c)

    def col_peer(i):
        return (r, lax.rem(c + i, n_col))

    barrier = pltpu.get_barrier_semaphore()

    def hello(dev):
        pl.semaphore_signal(barrier, inc=1, device_id=dev, device_id_type=MESH)

    each(1, n_col, lambda i: hello(col_peer(i)))
    pl.when(y_owner)(lambda: hello((4 * my_k + 2 * core + 1, chip)))
    each(1, n_row, lambda i: hello(plane_peer(i)))

    def rows(q):
        return pl.ds(q * sub, sub)

    loads = []
    for q in range(SUB):
        for at, (src, dst) in enumerate(((gate_hbm, gate), (hid_hbm, hid))):
            loads.append(pltpu.make_async_copy(src.at[rows(q)], dst.at[rows(q)], load_sem.at[2 * q + at]))
    for at, (src, dst) in enumerate(((tok_hbm, tok), (down_hbm, a_t), (adup_hbm, adup), (up_hbm, up))):
        loads.append(pltpu.make_async_copy(src, dst, load_sem.at[2 * SUB + at]))
    for load in loads:
        load.start()

    def ring(way, s, h):
        if way == 0:
            block, dev = lax.rem(c - s + n_col, n_col), (r, right)
        else:
            block, dev = lax.rem(c + s, n_col), (r, left)
        part = gbuf.at[block, h]
        return rcopy(part, part, ring_send.at[way, s, h], ring_recv.at[way, s, h], dev)

    for q in range(SUB):
        loads[2 * q].wait()
        loads[2 * q + 1].wait()
        v = gate[rows(q), :].astype(F32)
        gbuf[c, q] = (hid[rows(q), :].astype(F32) * (v / (1.0 + jnp.exp(-v)))).astype(BF16)
        if q == 0:
            pl.when(odd)(lambda: pl.semaphore_wait(barrier, n_col + n_row - 1))
            pl.when(jnp.logical_not(odd))(lambda: pl.semaphore_wait(barrier, n_col + n_row - 2))
        for way in range(2):
            ring(way, 0, q).start()

    gv = gates_ref[layer_ref[0]]
    for load in loads[2 * SUB :]:
        load.wait()

    zst[...] = fold_rows(dot_nt(split_rows(a_t[...]), tok[...])).astype(BF16).reshape(n_zp, 16, tr)

    def z1(k):
        @pl.when(z_gap * k != c)
        def _():
            small(zst.at[k], zrb.at[c], Z1, (r, z_gap * k)).start()

    each(0, n_zp, z1)
    y_part = fold_rows(dot_nt(split_rows(adup[...]), gbuf[c].reshape(2 * tr, fl)))
    for k in range(n_pc):
        for h in range(2):
            yst[2 * k + h] = y_part[8 * k : 8 * k + 8, h * tr : (h + 1) * tr]

    def y1(i):
        @pl.when(2 * i + 1 != r)
        def _():
            small(yst.at[i], yrb.at[r], Y1, (2 * i + 1, c)).start()

    each(0, 2 * n_pc, y1)

    def blocks_of(s):
        return (lax.rem(c - s + n_col, n_col), lax.rem(c + s, n_col))

    def tiles(v, put):
        for t in range(v.shape[0] // 16):
            for cg in range(cgs):
                put((t % tgs) * cgs + cg, t // tgs, v[16 * t : 16 * t + 16, 128 * cg : 128 * cg + 128])

    def multiply(group, parts, ours, theirs):
        def put_theirs(owner, at, v):
            xst[group, owner, at] = v.astype(BF16)

        def put_ours(owner, at, v):
            keep[owner, at] = v

        tiles(dot_nn(theirs, wbuf[...]), put_theirs)
        out, into = xst.at[group, :, pl.ds(0, parts)], xrb.at[group, :, pl.ds(0, parts)]
        rcopy(out, into, x_send.at[group], x_recv.at[group], (r + 1 - 2 * core, c)).start()
        tiles(dot_nn(ours, wbuf[...]), put_ours)

    def halves(block):
        def one(h):
            return jnp.concatenate([gbuf[block, 2 * h], gbuf[block, 2 * h + 1]], axis=0)

        return one(core), one(1 - core)

    def multiply_pair(s):
        ups, downs = blocks_of(s)
        up_ours, up_theirs = halves(ups)
        down_ours, down_theirs = halves(downs)
        multiply(
            s,
            4,
            jnp.concatenate([up_ours, down_ours], axis=0),
            jnp.concatenate([up_theirs, down_theirs], axis=0),
        )

    def scatter(group, parts):
        into = xrb.at[group, :, pl.ds(0, parts)]
        rcopy(into, into, x_send.at[group], x_recv.at[group], (r + 1 - 2 * core, c)).wait_recv()

        def add(p):
            both = keep[p, pl.ds(0, parts)] + xrb[group, p, pl.ds(0, parts)].astype(F32)
            stage[group, p, pl.ds(0, parts)] = both.astype(BF16)

        each(0, n_chip, add)

        def send(i):
            p = lax.rem(chip + i, n_chip)
            rcopy(
                stage.at[group, p, pl.ds(0, parts)],
                rbuf.at[group, chip, pl.ds(0, parts)],
                rs_send.at[group],
                rs_recv.at[group],
                (2 * p + core, c),
            ).start()

        each(1, n_chip, send)
        rbuf[group, chip, pl.ds(0, parts)] = stage[group, chip, pl.ds(0, parts)]

    def reduce(group, parts, pieces):
        got = rbuf.at[group, pl.ds(0, n_chip - 1), pl.ds(0, parts)]
        rcopy(got, got, rs_send.at[group], rs_recv.at[group], (r, right)).wait_recv()

        def add(i, acc):
            return acc + rbuf[group, i, pl.ds(0, parts)].astype(F32)

        total = lax.fori_loop(0, n_chip, add, jnp.zeros((parts, 16, 128), F32))
        ost[group, pl.ds(0, parts)] = total.astype(BF16)
        for at, size, block, place in pieces:

            @pl.when(block != chip)
            def _():
                small(
                    ost.at[group, pl.ds(at, size)],
                    fin.at[chip, pl.ds(place, size)],
                    FIN,
                    (2 * block + core, c),
                ).start()

            @pl.when(block == chip)
            def _():
                fin[chip, pl.ds(place, size)] = ost[group, pl.ds(at, size)]

    def reduce_pair(s):
        ups, downs = blocks_of(s)
        reduce(s, 4, ((0, 2, ups, 0), (2, 2, downs, 0)))

    def weights_and_own():
        for i in range(fl // QBLOCK):
            for j in range(dl // QBLOCK):
                at = (pl.ds(i * QBLOCK, QBLOCK), pl.ds(j * QBLOCK, QBLOCK))
                wbuf[at] = (up[at].astype(F32) * scale_ref[j, i]).astype(BF16)
        ours, theirs = halves(c)
        multiply(0, 2, ours, theirs)

    def to_column(ref, which):
        each(1, n_col, lambda i: small(ref, ref, which, col_peer(i)).start())

    def wait_pieces(which, owner, count, ref):
        @pl.when(owner)
        def _():
            if count > 1:
                wait_small(which, ref.at[pl.ds(0, count - 1)])

        pl.when(jnp.logical_not(owner))(lambda: wait_small(which, ref))

    def z_sum():
        @pl.when(z_owner)
        def _():
            zrb[c] = zst[my_z]
            wait_small(Z1, zrb.at[pl.ds(0, n_col - 1)])
            zfull[r, my_z] = jnp.sum(zrb[...].astype(F32), axis=0).astype(BF16)
            to_column(zfull.at[r, my_z], Z2)

    def z_plane():
        wait_pieces(Z2, z_owner, n_zp, zfull.at[r])
        each(1, n_row, lambda i: small(zfull.at[r], zfull.at[r], Z3, plane_peer(i)).start())

    def z_ready():
        wait_small(Z3, zfull.at[pl.ds(0, n_row - 1)])

        def join(b):
            zcat[b] = jnp.concatenate(
                [zfull[2 * b].reshape(rank, tr), zfull[2 * b + 1].reshape(rank, tr)], axis=1
            )

        each(0, n_col, join)

    def y_sum():
        @pl.when(odd)
        def _():
            yrb[r] = yst[chip]
            wait_small(Y1, yrb.at[pl.ds(0, n_row - 1)])
            y2st[...] = jnp.sum(yrb[...], axis=0)
            k = lax.div(chip, 2)
            small(y2st, yt.at[k], Y2, (2 * c + lax.rem(chip, 2), 2 * k)).start()

    def y_column():
        @pl.when(y_owner)
        def _():
            wait_small(Y2, yt.at[my_k])
            to_column(yt.at[my_k], Y3)

    def up_block(b):
        gpart[b] = dot_nn(zcat[b], gbuf[b].reshape(2 * tr, fl))

    def down_part():
        wait_pieces(Y3, y_owner, n_pc, yt)
        gd_t = fold_rows(dot_nn(split_rows(yt[...].reshape(rank, tr)), tok[...]))
        for k in range(n_pc):
            for q in range(cgs):
                gst[k * cgs + q] = gd_t[8 * k : 8 * k + 8, 128 * q : 128 * q + 128]

        def send(i):
            j = lax.rem(r + i, n_row)
            small(gst.at[j], grb.at[r], D1, (j, c)).start()

        each(1, n_row, send)
        grb[r] = gst[r]

    def make_lora():
        y_s = split_rows(yt[...].reshape(rank, tr))
        a_s = split_rows(a_t[...])
        y_left = jnp.concatenate([y_s[:rank], y_s[:rank], y_s[rank:]], axis=0).astype(F32).T.astype(BF16)
        a_right = jnp.concatenate([a_s[:rank], a_s[rank:], a_s[:rank]], axis=0)
        lora[...] = gv * dot_nn(y_left, a_right)

    def down_sum():
        wait_small(D1, grb.at[pl.ds(0, n_row - 1)])
        gfull[r] = jnp.sum(grb[...], axis=0)
        each(1, n_row, lambda i: small(gfull.at[r], gfull.at[r], D2, plane_peer(i)).start())

    def down_ready():
        wait_small(D2, gfull.at[pl.ds(0, n_row - 1)])
        strips = []
        for k in range(n_pc):
            strips.append(jnp.concatenate([gfull[k * cgs + q] for q in range(cgs)], axis=1))
        gd_t = jnp.concatenate(strips, axis=0)
        gd_ref[...] = gv * gd_t
        srb[c] = jnp.full(srb.shape[1:], jnp.sum(gd_t * a_t[...]), F32)

        to_column_gate()

    def to_column_gate():
        each(1, n_col, lambda i: small(srb.at[c], srb.at[c], S1, col_peer(i)).start())

    def gate_done():
        wait_small(S1, srb.at[pl.ds(0, n_col - 1)])
        gg_ref[0, 0] = jnp.sum(jnp.sum(srb[...], axis=0)[:, 0:1])

    up_at = 20

    def work(n):
        s, h = 1 + lax.div(n, SUB), lax.rem(n, SUB)
        pl.when(n == 0)(weights_and_own)
        @pl.when(jnp.logical_and(h == 1, s < half))
        def _():
            pl.when(s == 1)(lambda: scatter(0, 2))
            pl.when(s > 1)(lambda: scatter(s - 1, 4))

        @pl.when(jnp.logical_and(h == 3, s < half))
        def _():
            multiply_pair(s)
            pl.when(s == 1)(lambda: reduce(0, 2, ((0, 2, c, 0),)))
            pl.when(s > 1)(lambda: reduce_pair(s - 1))

        pl.when(n == 3)(y_sum)
        pl.when(n == 6)(z_sum)
        pl.when(n == 8)(y_column)
        pl.when(n == 11)(z_plane)
        pl.when(n == 13)(down_part)
        pl.when(n == 14)(make_lora)
        pl.when(n == 15)(z_ready)
        pl.when(n == 16)(down_sum)
        pl.when(n == 18)(down_ready)
        pl.when(n == 26)(gate_done)

        @pl.when(jnp.logical_and(n >= up_at, n < up_at + half))
        def _():
            ups, downs = blocks_of(n - up_at)
            up_block(ups)
            pl.when(n > up_at)(lambda: up_block(downs))

    def slot(n):
        s, h = 1 + lax.div(n, SUB), lax.rem(n, SUB)
        ring(0, s - 1, h).wait_recv()
        pl.when(jnp.logical_or(s < half - 1, h < SUB // 2))(lambda: ring(0, s, h).start())
        ring(1, s - 1, h).wait_recv()
        pl.when(jnp.logical_or(s < half - 1, h >= SUB // 2))(lambda: ring(1, s, h).start())
        work(n)

    slots = SUB * (half - 1)
    each(0, slots, slot)
    last = up_at + 8
    if last > slots:
        each(slots, last, work)

    far = lax.rem(c + half, n_col)
    scatter(half - 1, 4)
    for t in range(2):
        ring(0, half - 1, t).wait_recv()
        ring(1, half - 1, t + 2).wait_recv()
        multiply(half + t, 1, gbuf[far, 2 * core + t], gbuf[far, 2 - 2 * core + t])
        scatter(half + t, 1)
    up_block(far)
    reduce_pair(half - 1)
    reduce(half, 1, ((0, 1, far, 0),))
    acc = gpart[0]
    for b in range(1, n_col):
        acc = acc + gpart[b]
    gu_ref[...] = gv * acc
    reduce(half + 1, 1, ((0, 1, far, 1),))
    wait_small(FIN, fin.at[pl.ds(0, n_chip - 1)])
    for p in range(n_chip):
        for at in range(2):
            here = (pl.ds(16 * (tgs * at + p // cgs), 16), pl.ds(128 * (p % cgs), 128))
            gi_ref[here] = (fin[p, at].astype(F32) + lora[here]).astype(BF16)

    def drain(s):
        for way in range(2):
            for h in range(SUB):
                if (way == 0) == (h < SUB // 2):
                    ring(way, s, h).wait_send()
                else:
                    pl.when(s < half - 1)(lambda: ring(way, s, h).wait_send())

    each(0, half, drain)

    def sent_group(group, parts):
        out = xst.at[group, :, pl.ds(0, parts)]
        rcopy(out, out, x_send.at[group], x_recv.at[group], (r, right)).wait_send()
        out = stage.at[group, pl.ds(0, n_chip - 1), pl.ds(0, parts)]
        rcopy(out, out, rs_send.at[group], rs_recv.at[group], (r, right)).wait_send()

    sent_group(0, 2)
    each(1, half, lambda s: sent_group(s, 4))
    sent_group(half, 1)
    sent_group(half + 1, 1)

    @pl.when(odd)
    def _():
        sent(Y1, yst.at[pl.ds(0, 2 * n_pc - 1)])
        sent(Y2, y2st)

    pl.when(jnp.logical_not(odd))(lambda: sent(Y1, yst))

    @pl.when(z_owner)
    def _():
        if n_zp > 1:
            sent(Z1, zst.at[pl.ds(0, n_zp - 1)])
        sent(Z2, zrb.at[pl.ds(0, n_col - 1)])

    pl.when(jnp.logical_not(z_owner))(lambda: sent(Z1, zst))
    pl.when(y_owner)(lambda: sent(Y3, yrb.at[pl.ds(0, n_col - 1)]))
    sent(S1, srb.at[pl.ds(0, n_col - 1)])
    sent(Z3, zfull.at[pl.ds(0, n_row - 1)])
    sent(D1, gst.at[pl.ds(0, n_row - 1)])
    sent(D2, gfull.at[pl.ds(0, n_row - 1)])
    sent(FIN, fin.at[pl.ds(0, n_chip - 1)])


def per_device(
    n_row,
    n_col,
    tokens,
    gate_pre,
    grad_hidden,
    up_values,
    up_scales,
    adapter_down,
    adapter_up,
    layer_gates,
    layer,
):
    tr, dl = tokens.shape
    fl = up_values.shape[0]
    rank = adapter_down.shape[1]
    n_pc = rank // 8
    n_chip = n_row // 2
    half = n_col // 2
    groups = half + 2
    hbm = pl.BlockSpec(memory_space=pltpu.HBM)
    vmem = pl.BlockSpec(memory_space=pltpu.VMEM)
    smem = pl.BlockSpec(memory_space=pltpu.SMEM)
    outs = pl.pallas_call(
        functools.partial(kernel, n_row, n_col),
        out_shape=(
            jax.ShapeDtypeStruct((tr, dl), BF16),
            jax.ShapeDtypeStruct((rank, dl), F32),
            jax.ShapeDtypeStruct((rank, fl), F32),
            jax.ShapeDtypeStruct((1, 1), F32),
        ),
        in_specs=[hbm, hbm, hbm, hbm, smem, hbm, hbm, smem, smem],
        out_specs=(vmem, vmem, vmem, smem),
        scratch_shapes=[
            pltpu.VMEM((tr, dl), BF16),
            pltpu.VMEM((2 * tr, fl), BF16),
            pltpu.VMEM((2 * tr, fl), BF16),
            pltpu.VMEM((fl, dl), BF16),
            pltpu.VMEM((rank, dl), F32),
            pltpu.VMEM((rank, fl), F32),
            pltpu.VMEM((n_col, SUB, 2 * tr // SUB, fl), BF16),
            pltpu.VMEM((fl, dl), BF16),
            pltpu.VMEM((n_chip, 4, 16, 128), F32),
            pltpu.VMEM((groups, n_chip, 4, 16, 128), BF16),
            pltpu.VMEM((groups, n_chip, 4, 16, 128), BF16),
            pltpu.VMEM((groups, n_chip, 4, 16, 128), BF16),
            pltpu.VMEM((groups, n_chip, 4, 16, 128), BF16),
            pltpu.VMEM((groups, 4, 16, 128), BF16),
            pltpu.VMEM((n_chip, 2, 16, 128), BF16),
            pltpu.VMEM((tr, dl), F32),
            pltpu.VMEM((rank // 16, 16, tr), BF16),
            pltpu.VMEM((n_col, 16, tr), BF16),
            pltpu.VMEM((n_row, rank // 16, 16, tr), BF16),
            pltpu.VMEM((n_col, rank, 2 * tr), BF16),
            pltpu.VMEM((n_col, rank, fl), F32),
            pltpu.VMEM((2 * n_pc, 8, tr), F32),
            pltpu.VMEM((n_row, 8, tr), F32),
            pltpu.VMEM((8, tr), F32),
            pltpu.VMEM((n_pc, 8, tr), F32),
            pltpu.VMEM((n_row, 8, 128), F32),
            pltpu.VMEM((n_row, 8, 128), F32),
            pltpu.VMEM((n_row, 8, 128), F32),
            pltpu.VMEM((n_col, 1, 128), F32),
            pltpu.SemaphoreType.DMA((2 * SUB + 4,)),
            pltpu.SemaphoreType.DMA((2, half, SUB)),
            pltpu.SemaphoreType.DMA((2, half, SUB)),
            pltpu.SemaphoreType.DMA((groups,)),
            pltpu.SemaphoreType.DMA((groups,)),
            pltpu.SemaphoreType.DMA((groups,)),
            pltpu.SemaphoreType.DMA((groups,)),
            pltpu.SemaphoreType.DMA((10,)),
            pltpu.SemaphoreType.DMA((10,)),
        ],
        compiler_params=pltpu.CompilerParams(
            collective_id=0, has_side_effects=True, vmem_limit_bytes=56 * 1024 * 1024
        ),
    )(
        tokens,
        gate_pre,
        grad_hidden,
        up_values,
        up_scales.T,
        adapter_down.T,
        adapter_up,
        layer_gates,
        layer,
    )
    grad_input, grad_down, grad_up, gate_grad = outs
    return grad_input, grad_down.T, grad_up, gate_grad.reshape(())


def solution(mesh):
    placed = (
        P("row", "col"),
        P("col", "row"),
        P("col", "row"),
        P("row", "col"),
        P("row", "col"),
        P("col", None),
        P(None, "row"),
        P(),
        P(),
    )
    return jax.shard_map(
        functools.partial(per_device, mesh.shape["row"], mesh.shape["col"]),
        mesh=mesh,
        in_specs=placed,
        out_specs=(P("row", "col"), P("col", None), P(None, "row"), P()),
        check_vma=False,
    )
```

time: 141 us -> 115 us (0.82)
  Pallas kernels: 130 us -> 109 us
  local copies, waits for them, and re-layouts: 7.17 us -> 2.97 us
    pallas_call x1, Pallas kernels: 130 us -> 109 us  [per_device(): pl.pallas_call(functools.partial(kernel, n_row, n_col), out_shape=(jax.Sh...]
    unnamed x17 -> x7, local copies, waits for them, and re-layouts: 7.17 us -> 2.97 us
where the time goes in v2:
time: 115 us
  Pallas kernels  109 us (95%)
  between operations  3 us (3%)
  local copies, waits for them, and re-layouts  2.97 us (3%)
    pallas_call x1, Pallas kernels, per_device(): pl.pallas_call(functools.partial(kernel, n_row, n_col), out_shape=(jax.Sh...  109 us
    unnamed x7, local copies, waits for them, and re-layouts  2.97 us

profile of v2, /device:TPU:4, one launch (start us, length us, event | category | flops | bytes accessed | tf_op | source)
XLA Modules:
  0.0 115.0 jit_solution(4366841438787576785)
XLA Ops:
  1.3 109.1 %shard_map.120 = (bf16[128,512]{1,0:T(8,128)(2,1)}, f32[64,512]{1,0:T(8,128)}, f32[64,896]{1,0:T(8,128)}, f32[1,1]{1,0:T(1,128)}) custom-call(bf16[128,512]{1,0:T(8,128)(2,1)} %tok_hbm.1, bf16[256,896]{1,0:T(8,128)(2,1)} %gate_hbm.1, bf16[256,896]{1,0:T(8,128)(2,1)} %hid_hbm.1, bf16[896,512]{1,0:T(8,128)(2,1)} %up_hbm.1, f32[4,7]{1,0:T(4,128)} %bitcast.6, ...), custom_call_target="tpu_custom_call" | custom-call | tf_op jit(solution)/shard_map/pallas_call | solution.py:531
  110.3 0.0 copy-start.1
  110.4 0.0 copy-start
  110.4 1.6 %copy.18 = bf16[128,512]{1,0:T(8,128)(2,1)} copy(bf16[128,512]{1,0:T(8,128)(2,1)} %get-tuple-element.16) | data formatting | bytes 262144
  112.0 0.0 copy-done.1
  112.0 0.7 copy.19
  112.6 0.0 copy-done
  112.6 0.7 copy.20
Async XLA Ops:
  110.3 1.6 %copy-start.1 = (f32[64,512]{1,0:T(8,128)S(1)}, f32[64,512]{1,0:T(8,128)}, u32[]{:S(2)}) copy-start(f32[64,512]{1,0:T(8,128)} %get-tuple-element.9) | copy-start | bytes 393220
  110.4 2.3 %copy-start = (f32[64,896]{1,0:T(8,128)S(1)}, f32[64,896]{1,0:T(8,128)}, u32[]{:S(2)}) copy-start(f32[64,896]{1,0:T(8,128)} %get-tuple-element.18) | copy-start | bytes 688132

commit v3 on v2

--- a/solution.py
+++ b/solution.py
@@ -12,7 +12,7 @@
 MESH = pl.DeviceIdType.MESH
 F32 = jnp.float32
 BF16 = jnp.bfloat16
-Z1, Z2, Z3, Y1, Y2, Y3, D1, D2, S1, FIN = range(10)
+Z1, Z2, Z3, Y1, Y2, YP, Y3, D1, D2, S1, FIN = range(11)
 
 
 def split_rows(v):
@@ -49,11 +49,11 @@
     gate_hbm,
     hid_hbm,
     up_hbm,
-    scale_ref,
+    scale_hbm,
     down_hbm,
     adup_hbm,
-    gates_ref,
-    layer_ref,
+    gates_hbm,
+    layer_hbm,
     gi_ref,
     gd_ref,
     gu_ref,
@@ -64,6 +64,9 @@
     up,
     a_t,
     adup,
+    scale_ref,
+    gates_ref,
+    layer_ref,
     gbuf,
     wbuf,
     keep,
@@ -82,6 +85,7 @@
     yst,
     yrb,
     y2st,
+    yall,
     yt,
     gst,
     grb,
@@ -96,6 +100,9 @@
     rs_recv,
     sm_send,
     sm_recv,
+    next_sem,
+    col_sem,
+    row0_sem,
 ):
     r = lax.axis_index("row")
     c = lax.axis_index("col")
@@ -140,13 +147,39 @@
         return (r, lax.rem(c + i, n_col))
 
     barrier = pltpu.get_barrier_semaphore()
-
-    def hello(dev):
-        pl.semaphore_signal(barrier, inc=1, device_id=dev, device_id_type=MESH)
-
-    each(1, n_col, lambda i: hello(col_peer(i)))
-    pl.when(y_owner)(lambda: hello((4 * my_k + 2 * core + 1, chip)))
-    each(1, n_row, lambda i: hello(plane_peer(i)))
+    first = c == 0
+
+    def turn(i):
+        late = jnp.where(i >= n_col - n_col // 4, half + n_col - 1 - i, i + n_col // 4)
+        return jnp.where(i < half, i, late)
+
+    my_turn = turn(c)
+    right_later, left_later = turn(right) > my_turn, turn(left) > my_turn
+
+    def hello(dev, sem=barrier):
+        pl.semaphore_signal(sem, inc=1, device_id=dev, device_id_type=MESH)
+
+    each(0, n_col, lambda i: pl.when(turn(i) > my_turn)(lambda: hello((r, i))))
+
+    @pl.when(r > 0)
+    def _():
+        each(1, n_row, lambda i: hello(plane_peer(i)))
+
+    def past_barrier():
+        pl.when(r > 0)(lambda: pl.semaphore_wait(barrier, my_turn + n_row - 2))
+
+        @pl.when(r == 0)
+        def _():
+            pl.semaphore_wait(barrier, my_turn + n_row - 1)
+            each(1, n_row, lambda i: hello((i, c), row0_sem))
+
+        pl.when(jnp.logical_not(left_later))(lambda: hello((r, left), next_sem.at[0]))
+        pl.when(jnp.logical_not(right_later))(lambda: hello((r, right), next_sem.at[1]))
+        each(0, n_col, lambda i: pl.when(turn(i) < my_turn)(lambda: hello((r, i), col_sem)))
+
+    def neighbours_in():
+        pl.when(right_later)(lambda: pl.semaphore_wait(next_sem.at[0], 1))
+        pl.when(jnp.logical_and(left_later, c > 0))(lambda: pl.semaphore_wait(next_sem.at[1], 1))
 
     def rows(q):
         return pl.ds(q * sub, sub)
@@ -155,7 +188,16 @@
     for q in range(SUB):
         for at, (src, dst) in enumerate(((gate_hbm, gate), (hid_hbm, hid))):
             loads.append(pltpu.make_async_copy(src.at[rows(q)], dst.at[rows(q)], load_sem.at[2 * q + at]))
-    for at, (src, dst) in enumerate(((tok_hbm, tok), (down_hbm, a_t), (adup_hbm, adup), (up_hbm, up))):
+    others = (
+        (tok_hbm, tok),
+        (down_hbm, a_t),
+        (adup_hbm, adup),
+        (up_hbm, up),
+        (scale_hbm, scale_ref),
+        (gates_hbm, gates_ref),
+        (layer_hbm, layer_ref),
+    )
+    for at, (src, dst) in enumerate(others):
         loads.append(pltpu.make_async_copy(src, dst, load_sem.at[2 * SUB + at]))
     for load in loads:
         load.start()
@@ -168,29 +210,23 @@
         part = gbuf.at[block, h]
         return rcopy(part, part, ring_send.at[way, s, h], ring_recv.at[way, s, h], dev)
 
+    past_barrier()
     for q in range(SUB):
         loads[2 * q].wait()
         loads[2 * q + 1].wait()
         v = gate[rows(q), :].astype(F32)
         gbuf[c, q] = (hid[rows(q), :].astype(F32) * (v / (1.0 + jnp.exp(-v)))).astype(BF16)
         if q == 0:
-            pl.when(odd)(lambda: pl.semaphore_wait(barrier, n_col + n_row - 1))
-            pl.when(jnp.logical_not(odd))(lambda: pl.semaphore_wait(barrier, n_col + n_row - 2))
-        for way in range(2):
-            ring(way, 0, q).start()
-
-    gv = gates_ref[layer_ref[0]]
+            neighbours_in()
+        ring(0, 0, q).start()
+        pl.when(jnp.logical_not(first))(lambda: ring(1, 0, q).start())
+
     for load in loads[2 * SUB :]:
         load.wait()
+    gv = gates_ref[layer_ref[0]]
 
     zst[...] = fold_rows(dot_nt(split_rows(a_t[...]), tok[...])).astype(BF16).reshape(n_zp, 16, tr)
 
-    def z1(k):
-        @pl.when(z_gap * k != c)
-        def _():
-            small(zst.at[k], zrb.at[c], Z1, (r, z_gap * k)).start()
-
-    each(0, n_zp, z1)
     y_part = fold_rows(dot_nt(split_rows(adup[...]), gbuf[c].reshape(2 * tr, fl)))
     for k in range(n_pc):
         for h in range(2):
@@ -202,6 +238,13 @@
             small(yst.at[i], yrb.at[r], Y1, (2 * i + 1, c)).start()
 
     each(0, 2 * n_pc, y1)
+
+    @pl.when(first)
+    def _():
+        pl.semaphore_wait(next_sem.at[1], 1)
+        for q in range(SUB):
+            ring(1, 0, q).start()
+
 
     def blocks_of(s):
         return (lax.rem(c - s + n_col, n_col), lax.rem(c + s, n_col))
@@ -292,6 +335,7 @@
         reduce(s, 4, ((0, 2, ups, 0), (2, 2, downs, 0)))
 
     def weights_and_own():
+        pl.when(r > 0)(lambda: pl.semaphore_wait(row0_sem, 1))
         for i in range(fl // QBLOCK):
             for j in range(dl // QBLOCK):
                 at = (pl.ds(i * QBLOCK, QBLOCK), pl.ds(j * QBLOCK, QBLOCK))
@@ -310,6 +354,15 @@
 
         pl.when(jnp.logical_not(owner))(lambda: wait_small(which, ref))
 
+    def z1(k):
+        @pl.when(z_gap * k != c)
+        def _():
+            small(zst.at[k], zrb.at[c], Z1, (r, z_gap * k)).start()
+
+    def z_start():
+        pl.when(my_turn < n_col - 1)(lambda: pl.semaphore_wait(col_sem, n_col - 1 - my_turn))
+        each(0, n_zp, z1)
+
     def z_sum():
         @pl.when(z_owner)
         def _():
@@ -339,12 +392,41 @@
             wait_small(Y1, yrb.at[pl.ds(0, n_row - 1)])
             y2st[...] = jnp.sum(yrb[...], axis=0)
             k = lax.div(chip, 2)
-            small(y2st, yt.at[k], Y2, (2 * c + lax.rem(chip, 2), 2 * k)).start()
+            dest = 2 * c + lax.rem(chip, 2)
+
+            @pl.when(dest != r)
+            def _():
+                small(y2st, yall.at[k], Y2, (dest, c)).start()
+
+            @pl.when(dest == r)
+            def _():
+                yall[k] = y2st[...]
+
+    def y_root():
+        @pl.when(chip == c)
+        def _():
+            @pl.when(lax.rem(r, 4) == 3)
+            def _():
+                if n_pc > 1:
+                    wait_small(Y2, yall.at[pl.ds(0, n_pc - 1)])
+
+            pl.when(lax.rem(r, 4) != 3)(lambda: wait_small(Y2, yall))
+
+            def part(k):
+                @pl.when(2 * k != c)
+                def _():
+                    small(yall.at[k], yt.at[k], YP, (r, 2 * k)).start()
+
+                @pl.when(2 * k == c)
+                def _():
+                    yt[k] = yall[k]
+
+            each(0, n_pc, part)
 
     def y_column():
         @pl.when(y_owner)
         def _():
-            wait_small(Y2, yt.at[my_k])
+            pl.when(chip != c)(lambda: wait_small(YP, yt.at[my_k]))
             to_column(yt.at[my_k], Y3)
 
     def up_block(b):
@@ -394,7 +476,7 @@
         wait_small(S1, srb.at[pl.ds(0, n_col - 1)])
         gg_ref[0, 0] = jnp.sum(jnp.sum(srb[...], axis=0)[:, 0:1])
 
-    up_at = 20
+    up_at = 24
 
     def work(n):
         s, h = 1 + lax.div(n, SUB), lax.rem(n, SUB)
@@ -404,35 +486,49 @@
             pl.when(s == 1)(lambda: scatter(0, 2))
             pl.when(s > 1)(lambda: scatter(s - 1, 4))
 
+        @pl.when(jnp.logical_and(h == 0, jnp.logical_and(s > 1, s < half)))
+        def _():
+            pl.when(s == 2)(lambda: reduce(0, 2, ((0, 2, c, 0),)))
+            pl.when(s > 2)(lambda: reduce_pair(s - 2))
+
         @pl.when(jnp.logical_and(h == 3, s < half))
         def _():
             multiply_pair(s)
-            pl.when(s == 1)(lambda: reduce(0, 2, ((0, 2, c, 0),)))
-            pl.when(s > 1)(lambda: reduce_pair(s - 1))
-
-        pl.when(n == 3)(y_sum)
-        pl.when(n == 6)(z_sum)
-        pl.when(n == 8)(y_column)
-        pl.when(n == 11)(z_plane)
-        pl.when(n == 13)(down_part)
-        pl.when(n == 14)(make_lora)
-        pl.when(n == 15)(z_ready)
-        pl.when(n == 16)(down_sum)
-        pl.when(n == 18)(down_ready)
-        pl.when(n == 26)(gate_done)
-
-        @pl.when(jnp.logical_and(n >= up_at, n < up_at + half))
-        def _():
-            ups, downs = blocks_of(n - up_at)
-            up_block(ups)
-            pl.when(n > up_at)(lambda: up_block(downs))
+
+        pl.when(n == 2)(y_sum)
+        pl.when(n == 5)(z_start)
+        pl.when(n == 5)(y_root)
+        pl.when(n == 13)(z_sum)
+        pl.when(n == 11)(y_column)
+        pl.when(n == 20)(z_plane)
+        pl.when(n == 18)(down_part)
+        pl.when(n == 19)(make_lora)
+        pl.when(n == 23)(z_ready)
+        pl.when(n == 22)(down_sum)
+        pl.when(n == 26)(down_ready)
+
+        @pl.when(jnp.logical_and(n >= up_at, n < up_at + half // 2))
+        def _():
+            def group(i):
+                ups, downs = blocks_of(2 * (n - up_at) + i)
+                up_block(ups)
+                pl.when(n + i > up_at)(lambda: up_block(downs))
+
+            each(0, 2, group)
+
+    def brings(way, h, at):
+        split = jnp.where(at == 0, 0, SUB // 2)
+        return h < split if way == 0 else h >= split
+
+    def sends(way, h):
+        return brings(way, h, right if way == 0 else left)
 
     def slot(n):
         s, h = 1 + lax.div(n, SUB), lax.rem(n, SUB)
         ring(0, s - 1, h).wait_recv()
-        pl.when(jnp.logical_or(s < half - 1, h < SUB // 2))(lambda: ring(0, s, h).start())
+        pl.when(jnp.logical_or(s < half - 1, sends(0, h)))(lambda: ring(0, s, h).start())
         ring(1, s - 1, h).wait_recv()
-        pl.when(jnp.logical_or(s < half - 1, h >= SUB // 2))(lambda: ring(1, s, h).start())
+        pl.when(jnp.logical_or(s < half - 1, sends(1, h)))(lambda: ring(1, s, h).start())
         work(n)
 
     slots = SUB * (half - 1)
@@ -443,9 +539,11 @@
 
     far = lax.rem(c + half, n_col)
     scatter(half - 1, 4)
+    reduce_pair(half - 2)
     for t in range(2):
-        ring(0, half - 1, t).wait_recv()
-        ring(1, half - 1, t + 2).wait_recv()
+        for h in (t, t + 2):
+            pl.when(brings(0, h, c))(lambda: ring(0, half - 1, h).wait_recv())
+            pl.when(brings(1, h, c))(lambda: ring(1, half - 1, h).wait_recv())
         multiply(half + t, 1, gbuf[far, 2 * core + t], gbuf[far, 2 - 2 * core + t])
         scatter(half + t, 1)
     up_block(far)
@@ -455,53 +553,61 @@
     for b in range(1, n_col):
         acc = acc + gpart[b]
     gu_ref[...] = gv * acc
+    def drain(s):
+        for way in range(2):
+            for h in range(SUB):
+                pl.when(jnp.logical_or(s < half - 1, sends(way, h)))(lambda: ring(way, s, h).wait_send())
+
+    each(0, half, drain)
+
+    def sent_group(group, parts):
+        out = xst.at[group, :, pl.ds(0, parts)]
+        rcopy(out, out, x_send.at[group], x_recv.at[group], (r, right)).wait_send()
+        out = stage.at[group, pl.ds(0, n_chip - 1), pl.ds(0, parts)]
+        rcopy(out, out, rs_send.at[group], rs_recv.at[group], (r, right)).wait_send()
+
+    sent_group(0, 2)
+    each(1, half, lambda s: sent_group(s, 4))
+    sent_group(half, 1)
+
+    @pl.when(odd)
+    def _():
+        sent(Y1, yst.at[pl.ds(0, 2 * n_pc - 1)])
+        dest = 2 * c + lax.rem(chip, 2)
+        pl.when(dest != r)(lambda: sent(Y2, y2st))
+
+    @pl.when(chip == c)
+    def _():
+        @pl.when(y_owner)
+        def _():
+            if n_pc > 1:
+                sent(YP, yall.at[pl.ds(0, n_pc - 1)])
+
+        pl.when(jnp.logical_not(y_owner))(lambda: sent(YP, yall))
+
+    pl.when(jnp.logical_not(odd))(lambda: sent(Y1, yst))
+
+    @pl.when(z_owner)
+    def _():
+        if n_zp > 1:
+            sent(Z1, zst.at[pl.ds(0, n_zp - 1)])
+        sent(Z2, zrb.at[pl.ds(0, n_col - 1)])
+
+    pl.when(jnp.logical_not(z_owner))(lambda: sent(Z1, zst))
+    pl.when(y_owner)(lambda: sent(Y3, yrb.at[pl.ds(0, n_col - 1)]))
+    sent(S1, srb.at[pl.ds(0, n_col - 1)])
+    sent(Z3, zfull.at[pl.ds(0, n_row - 1)])
+    sent(D1, gst.at[pl.ds(0, n_row - 1)])
+    sent(D2, gfull.at[pl.ds(0, n_row - 1)])
+
     reduce(half + 1, 1, ((0, 1, far, 1),))
     wait_small(FIN, fin.at[pl.ds(0, n_chip - 1)])
     for p in range(n_chip):
         for at in range(2):
             here = (pl.ds(16 * (tgs * at + p // cgs), 16), pl.ds(128 * (p % cgs), 128))
             gi_ref[here] = (fin[p, at].astype(F32) + lora[here]).astype(BF16)
-
-    def drain(s):
-        for way in range(2):
-            for h in range(SUB):
-                if (way == 0) == (h < SUB // 2):
-                    ring(way, s, h).wait_send()
-                else:
-                    pl.when(s < half - 1)(lambda: ring(way, s, h).wait_send())
-
-    each(0, half, drain)
-
-    def sent_group(group, parts):
-        out = xst.at[group, :, pl.ds(0, parts)]
-        rcopy(out, out, x_send.at[group], x_recv.at[group], (r, right)).wait_send()
-        out = stage.at[group, pl.ds(0, n_chip - 1), pl.ds(0, parts)]
-        rcopy(out, out, rs_send.at[group], rs_recv.at[group], (r, right)).wait_send()
-
-    sent_group(0, 2)
-    each(1, half, lambda s: sent_group(s, 4))
-    sent_group(half, 1)
+    gate_done()
     sent_group(half + 1, 1)
-
-    @pl.when(odd)
-    def _():
-        sent(Y1, yst.at[pl.ds(0, 2 * n_pc - 1)])
-        sent(Y2, y2st)
-
-    pl.when(jnp.logical_not(odd))(lambda: sent(Y1, yst))
-
-    @pl.when(z_owner)
-    def _():
-        if n_zp > 1:
-            sent(Z1, zst.at[pl.ds(0, n_zp - 1)])
-        sent(Z2, zrb.at[pl.ds(0, n_col - 1)])
-
-    pl.when(jnp.logical_not(z_owner))(lambda: sent(Z1, zst))
-    pl.when(y_owner)(lambda: sent(Y3, yrb.at[pl.ds(0, n_col - 1)]))
-    sent(S1, srb.at[pl.ds(0, n_col - 1)])
-    sent(Z3, zfull.at[pl.ds(0, n_row - 1)])
-    sent(D1, gst.at[pl.ds(0, n_row - 1)])
-    sent(D2, gfull.at[pl.ds(0, n_row - 1)])
     sent(FIN, fin.at[pl.ds(0, n_chip - 1)])
 
 
@@ -536,7 +642,7 @@
             jax.ShapeDtypeStruct((rank, fl), F32),
             jax.ShapeDtypeStruct((1, 1), F32),
         ),
-        in_specs=[hbm, hbm, hbm, hbm, smem, hbm, hbm, smem, smem],
+        in_specs=[hbm] * 9,
         out_specs=(vmem, vmem, vmem, smem),
         scratch_shapes=[
             pltpu.VMEM((tr, dl), BF16),
@@ -545,6 +651,9 @@
             pltpu.VMEM((fl, dl), BF16),
             pltpu.VMEM((rank, dl), F32),
             pltpu.VMEM((rank, fl), F32),
+            pltpu.SMEM((dl // QBLOCK, fl // QBLOCK), F32),
+            pltpu.SMEM(layer_gates.shape, F32),
+            pltpu.SMEM((1,), jnp.int32),
             pltpu.VMEM((n_col, SUB, 2 * tr // SUB, fl), BF16),
             pltpu.VMEM((fl, dl), BF16),
             pltpu.VMEM((n_chip, 4, 16, 128), F32),
@@ -564,19 +673,23 @@
             pltpu.VMEM((n_row, 8, tr), F32),
             pltpu.VMEM((8, tr), F32),
             pltpu.VMEM((n_pc, 8, tr), F32),
+            pltpu.VMEM((n_pc, 8, tr), F32),
             pltpu.VMEM((n_row, 8, 128), F32),
             pltpu.VMEM((n_row, 8, 128), F32),
             pltpu.VMEM((n_row, 8, 128), F32),
             pltpu.VMEM((n_col, 1, 128), F32),
-            pltpu.SemaphoreType.DMA((2 * SUB + 4,)),
+            pltpu.SemaphoreType.DMA((2 * SUB + 7,)),
             pltpu.SemaphoreType.DMA((2, half, SUB)),
             pltpu.SemaphoreType.DMA((2, half, SUB)),
             pltpu.SemaphoreType.DMA((groups,)),
             pltpu.SemaphoreType.DMA((groups,)),
             pltpu.SemaphoreType.DMA((groups,)),
             pltpu.SemaphoreType.DMA((groups,)),
-            pltpu.SemaphoreType.DMA((10,)),
-            pltpu.SemaphoreType.DMA((10,)),
+            pltpu.SemaphoreType.DMA((11,)),
+            pltpu.SemaphoreType.DMA((11,)),
+            pltpu.SemaphoreType.REGULAR((2,)),
+            pltpu.SemaphoreType.REGULAR,
+            pltpu.SemaphoreType.REGULAR,
         ],
         compiler_params=pltpu.CompilerParams(
             collective_id=0, has_side_effects=True, vmem_limit_bytes=56 * 1024 * 1024

time: 115 us -> 112 us (0.974)
  Pallas kernels: 109 us -> 106 us
    pallas_call x1, Pallas kernels: 109 us -> 106 us  [per_device(): pl.pallas_call(functools.partial(kernel, n_row, n_col), out_shape=(jax.Sh...]
where the time goes in v3:
time: 112 us
  Pallas kernels  106 us (95%)
  between operations  3 us (3%)
  local copies, waits for them, and re-layouts  2.97 us (3%)
    pallas_call x1, Pallas kernels, per_device(): pl.pallas_call(functools.partial(kernel, n_row, n_col), out_shape=(jax.Sh...  106 us
    unnamed x7, local copies, waits for them, and re-layouts  2.97 us

profile of v3, /device:TPU:4, one launch (start us, length us, event | category | flops | bytes accessed | tf_op | source)
XLA Modules:
  0.0 112.3 jit_solution(16607930329096840437)
XLA Ops:
  1.3 106.3 %shard_map.120 = (bf16[128,512]{1,0:T(8,128)(2,1)}, f32[64,512]{1,0:T(8,128)}, f32[64,896]{1,0:T(8,128)}, f32[1,1]{1,0:T(1,128)}) custom-call(bf16[128,512]{1,0:T(8,128)(2,1)} %tok_hbm.1, bf16[256,896]{1,0:T(8,128)(2,1)} %gate_hbm.1, bf16[256,896]{1,0:T(8,128)(2,1)} %hid_hbm.1, bf16[896,512]{1,0:T(8,128)(2,1)} %up_hbm.1, f32[4,7]{1,0:T(4,128)} %bitcast.6, ...), custom_call_target="tpu_custom_call" | custom-call | tf_op jit(solution)/shard_map/pallas_call | solution.py:637
  107.6 0.0 copy-start.1
  107.6 0.0 copy-start
  107.6 1.6 %copy.18 = bf16[128,512]{1,0:T(8,128)(2,1)} copy(bf16[128,512]{1,0:T(8,128)(2,1)} %get-tuple-element.16) | data formatting | bytes 262144
  109.2 0.0 copy-done.1
  109.2 0.7 copy.19
  109.9 0.0 copy-done
  109.9 0.7 copy.20
Async XLA Ops:
  107.6 1.6 %copy-start.1 = (f32[64,512]{1,0:T(8,128)S(1)}, f32[64,512]{1,0:T(8,128)}, u32[]{:S(2)}) copy-start(f32[64,512]{1,0:T(8,128)} %get-tuple-element.9) | copy-start | bytes 393220
  107.6 2.3 %copy-start = (f32[64,896]{1,0:T(8,128)S(1)}, f32[64,896]{1,0:T(8,128)}, u32[]{:S(2)}) copy-start(f32[64,896]{1,0:T(8,128)} %get-tuple-element.18) | copy-start | bytes 688132

commit v4 on v3

--- a/solution.py
+++ b/solution.py
@@ -55,8 +55,8 @@
     gates_hbm,
     layer_hbm,
     gi_ref,
-    gd_ref,
-    gu_ref,
+    gd_hbm,
+    gu_hbm,
     gg_ref,
     tok,
     gate,
@@ -103,6 +103,9 @@
     next_sem,
     col_sem,
     row0_sem,
+    gd_ref,
+    gu_ref,
+    out_sem,
 ):
     r = lax.axis_index("row")
     c = lax.axis_index("col")
@@ -110,7 +113,7 @@
     chip = lax.div(r, 2)
     tr, dl = gi_ref.shape
     fl = wbuf.shape[0]
-    rank = gd_ref.shape[0]
+    rank = gd_hbm.shape[0]
     sub = 2 * tr // SUB
     n_pc = rank // 8
     n_chip = n_row // 2
@@ -125,6 +128,9 @@
     z_owner = lax.rem(c, z_gap) == 0
     y_owner = lax.rem(c, 2) == 0
     my_z, my_k = lax.div(c, z_gap), lax.div(c, 2)
+
+    gd_out = pltpu.make_async_copy(gd_ref, gd_hbm, out_sem.at[0])
+    gu_out = pltpu.make_async_copy(gu_ref, gu_hbm, out_sem.at[1])
 
     def rcopy(src, dst, ssem, rsem, dev):
         return pltpu.make_async_remote_copy(
@@ -465,6 +471,7 @@
             strips.append(jnp.concatenate([gfull[k * cgs + q] for q in range(cgs)], axis=1))
         gd_t = jnp.concatenate(strips, axis=0)
         gd_ref[...] = gv * gd_t
+        gd_out.start()
         srb[c] = jnp.full(srb.shape[1:], jnp.sum(gd_t * a_t[...]), F32)
 
         to_column_gate()
@@ -553,6 +560,7 @@
     for b in range(1, n_col):
         acc = acc + gpart[b]
     gu_ref[...] = gv * acc
+    gu_out.start()
     def drain(s):
         for way in range(2):
             for h in range(SUB):
@@ -609,6 +617,8 @@
     gate_done()
     sent_group(half + 1, 1)
     sent(FIN, fin.at[pl.ds(0, n_chip - 1)])
+    gd_out.wait()
+    gu_out.wait()
 
 
 def per_device(
@@ -643,7 +653,7 @@
             jax.ShapeDtypeStruct((1, 1), F32),
         ),
         in_specs=[hbm] * 9,
-        out_specs=(vmem, vmem, vmem, smem),
+        out_specs=(vmem, hbm, hbm, smem),
         scratch_shapes=[
             pltpu.VMEM((tr, dl), BF16),
             pltpu.VMEM((2 * tr, fl), BF16),
@@ -690,6 +700,9 @@
             pltpu.SemaphoreType.REGULAR((2,)),
             pltpu.SemaphoreType.REGULAR,
             pltpu.SemaphoreType.REGULAR,
+            pltpu.VMEM((rank, dl), F32),
+            pltpu.VMEM((rank, fl), F32),
+            pltpu.SemaphoreType.DMA((2,)),
         ],
         compiler_params=pltpu.CompilerParams(
             collective_id=0, has_side_effects=True, vmem_limit_bytes=56 * 1024 * 1024

time: 112 us -> 112 us (level)
  no operation moved by 1% of the time
where the time goes in v4:
time: 112 us
  Pallas kernels  106 us (95%)
  between operations  3 us (3%)
  local copies, waits for them, and re-layouts  2.97 us (3%)
    pallas_call x1, Pallas kernels, per_device(): pl.pallas_call(functools.partial(kernel, n_row, n_col), out_shape=(jax.Sh...  106 us
    unnamed x7, local copies, waits for them, and re-layouts  2.97 us

profile of v4, /device:TPU:4, one launch (start us, length us, event | category | flops | bytes accessed | tf_op | source)
XLA Modules:
  0.0 112.2 jit_solution(13848088852824356732)
XLA Ops:
  1.3 106.2 %shard_map.120 = (bf16[128,512]{1,0:T(8,128)(2,1)}, f32[64,512]{1,0:T(8,128)}, f32[64,896]{1,0:T(8,128)}, f32[1,1]{1,0:T(1,128)}) custom-call(bf16[128,512]{1,0:T(8,128)(2,1)} %tok_hbm.1, bf16[256,896]{1,0:T(8,128)(2,1)} %gate_hbm.1, bf16[256,896]{1,0:T(8,128)(2,1)} %hid_hbm.1, bf16[896,512]{1,0:T(8,128)(2,1)} %up_hbm.1, f32[4,7]{1,0:T(4,128)} %bitcast.6, ...), custom_call_target="tpu_custom_call" | custom-call | tf_op jit(solution)/shard_map/pallas_call | solution.py:647
  107.5 0.0 copy-start.1
  107.5 0.0 copy-start
  107.5 1.6 %copy.18 = bf16[128,512]{1,0:T(8,128)(2,1)} copy(bf16[128,512]{1,0:T(8,128)(2,1)} %get-tuple-element.16) | data formatting | bytes 262144
  109.1 0.0 copy-done.1
  109.1 0.7 copy.19
  109.8 0.0 copy-done
  109.8 0.7 copy.20
Async XLA Ops:
  107.5 1.6 %copy-start.1 = (f32[64,512]{1,0:T(8,128)S(1)}, f32[64,512]{1,0:T(8,128)}, u32[]{:S(2)}) copy-start(f32[64,512]{1,0:T(8,128)} %get-tuple-element.9) | copy-start | bytes 393220
  107.5 2.3 %copy-start = (f32[64,896]{1,0:T(8,128)S(1)}, f32[64,896]{1,0:T(8,128)}, u32[]{:S(2)}) copy-start(f32[64,896]{1,0:T(8,128)} %get-tuple-element.18) | copy-start | bytes 688132
